TPU v7x, 512 devices: a whole 4x4x16 slice. The times are simulated.
512 devices in a mesh: replica: 32 (over x, z_lo, core), seq: 16 (over y, z_hi).
Axes of the slice: x: 4, y: 4, z: 16 (z_hi: 4, z_lo: 4; z = z_hi * 4 + z_lo), core: 2. Of those that a mesh axis runs over, the one named last changes fastest.
Arguments:
- query_rows: bfloat16 [32, 2048, 2048], P('replica', 'seq'), may hold values from -110 to 110, as said below
- key_rows: bfloat16 [32, 2048, 2048], P('replica', 'seq'), may hold values from -4 to 4
- value_rows: bfloat16 [32, 2048, 2048], P('replica', 'seq'), may hold values from -6 to 6
- out_grad: bfloat16 [32, 2048, 2048], P('replica', 'seq'), may hold values from -6 to 6
- drift: bfloat16 [32, 3072, 1536], P('replica', 'seq'), may hold values from -12 to 12
- kept_index: int32 [32, 48, 24, 32], P(None, 'seq'), may hold values from 0 to 4095, as said below
Outputs:
- query_grad: bfloat16 [32, 2048, 2048], P('replica', 'seq')
- key_grad: bfloat16 [32, 2048, 2048], P('replica', 'seq')
- value_grad: bfloat16 [32, 2048, 2048], P('replica', 'seq')
- outer_grad: bfloat16 [3072, 1536], P('seq')
Inputs may be any that keep to these rules, and one draw needn't show every extreme that they name: `query_rows`: queries follow a normal law clipped at 4 in the shown draw. `kept_index`: for each replica and block the j-th kept position (j from 0 to 31) lies in j * 64 * 2 to (j + 1) * 64 * 2 - 1; positions of one block are thus distinct and rising.
All inputs are finite; a program needn't handle non-finite values.
Results may differ from a plain program's by a relative error of at most 0.011.
Values may be sent and summed in bfloat16 or wider, within the bound.
A program may use at most 64 MiB of HBM per device.

v0:
```python
import math

import jax
import jax.numpy as jnp
from jax import lax
from jax.sharding import PartitionSpec as P

HEAD = 128
GROUP = 64
SEQS = 2


def dct_table(size):
    rows = jnp.arange(size)[:, None].astype(jnp.float32)
    cols = jnp.arange(size)[None, :].astype(jnp.float32)
    factor = jnp.where(rows == 0, jnp.sqrt(1.0 / size), jnp.sqrt(2.0 / size))
    return factor * jnp.cos(math.pi * (2.0 * cols + 1.0) * rows / (2.0 * size))


def forward_groups(field, table):
    nrow = field.shape[0] // GROUP
    ncol = field.shape[1] // GROUP
    rowed = jnp.einsum(
        "ij,ajc->aic",
        table,
        field.reshape(nrow, GROUP, field.shape[1]),
        precision=lax.Precision.HIGHEST,
    )
    both = jnp.einsum(
        "ajbk,lk->abjl",
        rowed.reshape(nrow, GROUP, ncol, GROUP),
        table,
        precision=lax.Precision.HIGHEST,
    )
    return both.reshape(nrow, ncol, GROUP * GROUP)


def inverse_groups(coeffs, table):
    nrow, ncol = (coeffs.shape[0], coeffs.shape[1])
    blocks = coeffs.reshape(nrow, ncol, GROUP, GROUP)
    first = jnp.einsum("abil,lk->aibk", blocks, table, precision=lax.Precision.HIGHEST)
    second = jnp.einsum("ij,aibk->ajbk", table, first, precision=lax.Precision.HIGHEST)
    return second.reshape(nrow * GROUP, ncol * GROUP)


def spread(values, index):
    nrow, ncol = (index.shape[-3], index.shape[-2])
    row_ix = jnp.arange(nrow, dtype=jnp.int32)[:, None, None]
    col_ix = jnp.arange(ncol, dtype=jnp.int32)[None, :, None]
    dense = jnp.zeros((nrow, ncol, GROUP * GROUP), jnp.float32)
    return dense.at[row_ix, col_ix, index].add(values)


def head_backward(query, keys_all, values_all, grads):
    length, hcount = (query.shape[0], query.shape[1])
    scale = 1.0 / math.sqrt(HEAD)
    block = min(512, length)
    nblock = length // block

    def step(carry, pieces):
        key_acc, value_acc = carry
        qpart, gpart = pieces
        scores = (
            jnp.einsum("qhd,khd->hqk", qpart, keys_all, preferred_element_type=jnp.float32) * scale
        )
        top = jnp.max(scores, axis=-1, keepdims=True)
        expo = jnp.exp(scores - top)
        probs = expo / jnp.sum(expo, axis=-1, keepdims=True)
        probs_low = probs.astype(jnp.bfloat16)
        attended = jnp.einsum(
            "hqk,khd->qhd", probs_low, values_all, preferred_element_type=jnp.float32
        )
        delta = jnp.transpose(jnp.sum(gpart.astype(jnp.float32) * attended, axis=-1))[:, :, None]
        pgrad = jnp.einsum("qhd,khd->hqk", gpart, values_all, preferred_element_type=jnp.float32)
        score_grad = (probs * (pgrad - delta)).astype(jnp.bfloat16)
        qgrad = (
            jnp.einsum("hqk,khd->qhd", score_grad, keys_all, preferred_element_type=jnp.float32)
            * scale
        )
        key_acc = (
            key_acc
            + jnp.einsum("hqk,qhd->khd", score_grad, qpart, preferred_element_type=jnp.float32)
            * scale
        )
        value_acc = value_acc + jnp.einsum(
            "hqk,qhd->khd", probs_low, gpart, preferred_element_type=jnp.float32
        )
        return ((key_acc, value_acc), qgrad.astype(jnp.bfloat16))

    start = jnp.zeros((length, hcount, HEAD), jnp.float32)
    (key_acc, value_acc), qgrads = lax.scan(
        step,
        (start, start),
        (query.reshape(nblock, block, hcount, HEAD), grads.reshape(nblock, block, hcount, HEAD)),
    )
    return (
        qgrads.reshape(length, hcount, HEAD),
        key_acc.astype(jnp.bfloat16),
        value_acc.astype(jnp.bfloat16),
    )


def window_backward(pieces):
    return head_backward(pieces[0], pieces[1], pieces[2], pieces[3])


def per_item(query, keys_all, values_all, grads):
    length, width = query.shape
    window = length // SEQS
    shaped = tuple(
        (a.reshape(SEQS, window, width // HEAD, HEAD) for a in (query, keys_all, values_all, grads))
    )
    qg, kg, vg = lax.map(window_backward, shaped)
    return (qg.reshape(length, width), kg.reshape(length, width), vg.reshape(length, width))


def head_work(pieces):
    return jax.vmap(per_item)(pieces[0], pieces[1], pieces[2], pieces[3])


def on_device(query_rows, key_rows, value_rows, out_grad, drift, kept_index):
    head_grads = head_work(
        (
            lax.all_to_all(query_rows, "seq", split_axis=2, concat_axis=1, tiled=True),
            lax.all_to_all(key_rows, "seq", split_axis=2, concat_axis=1, tiled=True),
            lax.all_to_all(value_rows, "seq", split_axis=2, concat_axis=1, tiled=True),
            lax.all_to_all(out_grad, "seq", split_axis=2, concat_axis=1, tiled=True),
        )
    )
    query_grad, key_grad, value_grad = (
        lax.all_to_all(head_grads[0], "seq", split_axis=1, concat_axis=2, tiled=True),
        lax.all_to_all(head_grads[1], "seq", split_axis=1, concat_axis=2, tiled=True),
        lax.all_to_all(head_grads[2], "seq", split_axis=1, concat_axis=2, tiled=True),
    )
    table = dct_table(GROUP)
    coeffs = forward_groups(drift[0].astype(jnp.float32), table)
    own_index = lax.dynamic_index_in_dim(kept_index, lax.axis_index("replica"), 0, keepdims=False)
    kept = jnp.take_along_axis(coeffs, own_index, axis=-1)
    total = lax.psum(spread(kept, own_index), "replica")
    outer_grad = inverse_groups(total, table).astype(jnp.bfloat16)
    return (query_grad, key_grad, value_grad, outer_grad)


def solution(mesh):
    placed = (
        P("replica", "seq", None),
        P("replica", "seq", None),
        P("replica", "seq", None),
        P("replica", "seq", None),
        P("replica", "seq", None),
        P(None, "seq", None, None),
    )
    return jax.shard_map(
        on_device,
        mesh=mesh,
        in_specs=placed,
        out_specs=(
            P("replica", "seq", None),
            P("replica", "seq", None),
            P("replica", "seq", None),
            P("seq", None),
        ),
        check_vma=False,
    )
```

profile of v0, /device:TPU:1, one launch (start us, length us, event | category | flops | bytes accessed | tf_op | source)
XLA Modules:
  0.0 718.0 jit_solution(11568504403392357051)
XLA Ops:
  7.2 2.4 copy.106
  10.2 11.5 %reduce.9 = bf16[2048,128]{1,0:T(8,128)(2,1)S(1)} reduce(bf16[2048,1,128]{2,1,0:T(2,128)(2,1)S(1)} %bitcast.232, bf16[]{:T(256)} %broadcast.159), dimensions={1}, to_apply=%bitcast.150.reduce_sub_computation | reduce | bytes 1048578
  22.6 18.4 %all-to-all-start = ((bf16[16,2,8192]{2,1,0:T(2,128)(2,1)}), bf16[16,2,8192]{2,1,0:T(2,128)(2,1)S(1)}, u32[]{:S(2)}, u32[]{:S(2)}) async-start(bf16[16,2,8192]{2,1,0:T(2,128)(2,1)} %reshape.223), calls=%async_computation | async-start | bytes 1048576 | tf_op jit(solution)/shard_map/all_to_all | solution.py:124
  41.8 11.6 %reduce.10 = bf16[2048,128]{1,0:T(8,128)(2,1)S(1)} reduce(bf16[2048,1,128]{2,1,0:T(2,128)(2,1)S(1)} %bitcast.236, bf16[]{:T(256)} %broadcast.159), dimensions={1}, to_apply=%bitcast.152.reduce_sub_computation | reduce | bytes 1048578
  54.2 13.9 %all-to-all-done = bf16[16,2,8192]{2,1,0:T(2,128)(2,1)S(1)} async-done(((bf16[16,2,8192]{2,1,0:T(2,128)(2,1)}), bf16[16,2,8192]{2,1,0:T(2,128)(2,1)S(1)}, u32[]{:S(2)}, u32[]{:S(2)}) %all-to-all-start) | async-done | bytes 524320 | tf_op jit(solution)/shard_map/all_to_all | solution.py:124
  68.1 9.0 %all-to-all-start.1 = ((bf16[16,2,8192]{2,1,0:T(2,128)(2,1)}), bf16[16,2,8192]{2,1,0:T(2,128)(2,1)S(1)}, u32[]{:S(2)}, u32[]{:S(2)}) async-start(bf16[16,2,8192]{2,1,0:T(2,128)(2,1)} %reshape.225), calls=%async_computation.1 | async-start | bytes 1048576 | tf_op jit(solution)/shard_map/all_to_all | solution.py:127
  77.9 11.5 %reduce.11 = bf16[2048,128]{1,0:T(8,128)(2,1)S(1)} reduce(bf16[2048,1,128]{2,1,0:T(2,128)(2,1)S(1)} %bitcast.237, bf16[]{:T(256)} %broadcast.159), dimensions={1}, to_apply=%bitcast.154.reduce_sub_computation | reduce | bytes 1048578
  90.3 7.2 all-to-all-done.1
  97.5 6.8 all-to-all-start.2
  104.3 2.4 copy.112
  106.6 12.3 %reduce.12 = bf16[2048,128]{1,0:T(8,128)(2,1)} reduce(bf16[2048,1,128]{2,1,0:T(2,128)(2,1)S(1)} %bitcast.238, bf16[]{:T(256)} %broadcast.159), dimensions={1}, to_apply=%bitcast.156.reduce_sub_computation | reduce | bytes 1048578
  119.0 2.0 reshape.229
  121.6 13.4 %all-to-all-start.3 = ((bf16[16,2,8192]{2,1,0:T(2,128)(2,1)}), bf16[16,2,8192]{2,1,0:T(2,128)(2,1)}, u32[]{:S(2)}, u32[]{:S(2)}) async-start(bf16[16,2,8192]{2,1,0:T(2,128)(2,1)} %reshape.229), calls=%async_computation.3 | async-start | bytes 1048576 | tf_op jit(solution)/shard_map/all_to_all | solution.py:126
  140.0 12.7 %all-to-all-done.3 = bf16[16,2,8192]{2,1,0:T(2,128)(2,1)} async-done(((bf16[16,2,8192]{2,1,0:T(2,128)(2,1)}), bf16[16,2,8192]{2,1,0:T(2,128)(2,1)}, u32[]{:S(2)}, u32[]{:S(2)}) %all-to-all-start.3) | async-done | bytes 524320 | tf_op jit(solution)/shard_map/all_to_all | solution.py:126
  152.7 2.2 reshape.230
  156.0 60.4 %while.30 = (s32[]{:T(128)}, bf16[2,1,1024,1,128]{4,2,3,1,0:T(8,128)(2,1)}, bf16[2,1,1024,1,128]{4,2,0,3,1:T(8,128)(2,1)}, bf16[2,1,1024,1,128]{4,2,0,3,1:T(8,12...) while((s32[]{:T(128)}, ...), condition=%wide.region_6.7_spmd, body=%wide.region_0.6_spmd.sunk | while | flops 813365760 | bytes 46414444 | solution.py:113
  156.0 1.8 constant_dynamic-slice_fusion.5
  157.7 1.8 dynamic-slice_bitcast_fusion.3
  159.5 21.8 %while.31 = (s32[]{:T(128)}, f32[1,1024,1,128]{1,3,2,0:T(8,128)}, f32[1,1024,1,128]{1,3,2,0:T(8,128)}, bf16[2,1,512,1,128]{4,2,3,1,0:T(8,128)(2,1)}, bf16[2,1,51...) while((s32[]{:T(128)}, f32[1,1024,1,128]{1,3,2,0:T(8,128)}, ...), condition=%wide.region_5.5_spmd.clone, body=%wide.region_1.4_spmd.clone.sunk | while | flops 813103616 | bytes 33831216 | solution.py:91
  159.5 1.5 multiply_reduce_fusion.3
  163.1 1.4 multiply_convert_fusion.2
  164.5 2.4 fusion.98
  168.2 1.4 fusion.100
  170.4 1.5 multiply_reduce_fusion.3
  174.0 1.4 multiply_convert_fusion.2
  175.4 2.6 fusion.98
  179.2 1.4 fusion.100
  181.4 1.8 constant_dynamic-update-slice_fusion.6
  186.2 1.8 constant_dynamic-slice_fusion.5
  187.9 1.8 dynamic-slice_bitcast_fusion.3
  189.7 21.8 %while.31 = (s32[]{:T(128)}, f32[1,1024,1,128]{1,3,2,0:T(8,128)}, f32[1,1024,1,128]{1,3,2,0:T(8,128)}, bf16[2,1,512,1,128]{4,2,3,1,0:T(8,128)(2,1)}, bf16[2,1,51...) while((s32[]{:T(128)}, f32[1,1024,1,128]{1,3,2,0:T(8,128)}, ...), condition=%wide.region_5.5_spmd.clone, body=%wide.region_1.4_spmd.clone.sunk | while | flops 813103616 | bytes 33831216 | solution.py:91
  189.7 1.5 multiply_reduce_fusion.3
  193.3 1.4 multiply_convert_fusion.2
  194.7 2.4 fusion.98
  198.4 1.4 fusion.100
  200.6 1.5 multiply_reduce_fusion.3
  204.1 1.4 multiply_convert_fusion.2
  205.6 2.6 fusion.98
  209.4 1.4 fusion.100
  211.5 1.8 constant_dynamic-update-slice_fusion.6
  216.4 1.8 copy.159
  218.2 11.6 %reduce.13 = bf16[2048,128]{1,0:T(8,128)(2,1)S(1)} reduce(bf16[2048,1,128]{2,1,0:T(2,128)(2,1)S(1)} %bitcast.234, bf16[]{:T(256)} %broadcast.159), dimensions={1}, to_apply=%bitcast.178.reduce_sub_computation | reduce | bytes 1048578
  230.7 3.8 all-to-all-start.4
  234.5 8.1 %copy.158 = bf16[1,2048,128]{2,0,1:T(2,128)(2,1)S(1)} copy(bf16[1,2048,128]{2,1,0:T(8,128)(2,1)S(1)} %bitcast.250) | data formatting | bytes 1048576 | tf_op jit(solution)/shard_map/vmap()/reshape;vmap()/transpose | solution.py:114
  242.6 11.5 %reduce.14 = bf16[2048,128]{1,0:T(8,128)(2,1)S(1)} reduce(bf16[2048,1,128]{2,1,0:T(2,128)(2,1)S(1)} %bitcast.235, bf16[]{:T(256)} %broadcast.159), dimensions={1}, to_apply=%bitcast.177.reduce_sub_computation | reduce | bytes 1048578
  255.1 14.4 %all-to-all-start.5 = ((bf16[16,2,8192]{2,1,0:T(2,128)(2,1)}), bf16[16,2,8192]{2,1,0:T(2,128)(2,1)}, u32[]{:S(2)}, u32[]{:S(2)}) async-start(bf16[16,2,8192]{2,1,0:T(2,128)(2,1)} %reshape.233), calls=%async_computation.5 | async-start | bytes 1048576 | tf_op jit(solution)/shard_map/all_to_all | solution.py:132
  270.6 1.8 convolution_bitcast_fusion.2
  272.4 1.7 reshape.192
  274.1 8.4 %fusion.29 = f32[3,24,64,64]{2,3,1,0:T(8,128)} fusion(f32[3,64,24,64]{3,2,1,0:T(8,128)S(1)} %reshape.192, f32[64]{0:T(128)S(1)} %iota_convert_fusion, f32[64]{0:T(128)S(1)} %get-tuple-element.267, f32[64]{0:T(128)S(1)} %get-tuple-element.266), kind=kOutput, calls=%fused_computation.49 | convolution fusion | flops 226504704 | bytes 2360064 | tf_op jit(solution)/shard_map/ajbk,lk->abjl/dot_general | solution.py:29
  282.5 3.0 copy.129
  285.5 2.2 reshape.193
  287.8 22.2 %gather_fusion = f32[2304]{0:T(1024)S(1)} fusion(f32[3,24,4096]{2,1,0:T(8,128)S(1)} %reshape.193, s32[2304]{0:T(1024)S(1)} %reshape.201), kind=kCustom, calls=%fused_computation | custom fusion | bytes 46080 | tf_op jit(solution)/shard_map/jit(take_along_axis)/gather | solution.py:138
  310.1 8.3 %copy.157 = bf16[1,2048,128]{2,0,1:T(2,128)(2,1)S(1)} copy(bf16[1,2048,128]{2,1,0:T(8,128)(2,1)S(1)} %bitcast.251) | data formatting | bytes 1048576 | tf_op jit(solution)/shard_map/vmap()/reshape;vmap()/transpose | solution.py:114
  318.4 11.5 %reduce.15 = bf16[2048,128]{1,0:T(8,128)(2,1)S(1)} reduce(bf16[2048,1,128]{2,1,0:T(2,128)(2,1)S(1)} %bitcast.233, bf16[]{:T(256)} %broadcast.159), dimensions={1}, to_apply=%bitcast.176.reduce_sub_computation | reduce | bytes 1048578
  330.8 14.0 %all-to-all-start.6 = ((bf16[16,2,8192]{2,1,0:T(2,128)(2,1)}), bf16[16,2,8192]{2,1,0:T(2,128)(2,1)}, u32[]{:S(2)}, u32[]{:S(2)}) async-start(bf16[16,2,8192]{2,1,0:T(2,128)(2,1)} %reshape.235), calls=%async_computation.6 | async-start | bytes 1048576 | tf_op jit(solution)/shard_map/all_to_all | solution.py:133
  345.8 15.7 %scatter_custom_fusion = f32[294912]{0:T(1024)S(1)} fusion(s32[2304]{0:T(1024)S(1)} %reshape.207, f32[2304]{0:T(1024)S(1)} %reshape.209, f32[]{:T(128)} %constant.54.clone.1), kind=kCustom, calls=%fused_computation.52 | custom fusion | flops 2304 | bytes 1179652
  361.4 1.8 reshape.194
  363.2 324.8 %all-reduce.2.cloned.1.call-done = f32[3,24,64,64]{3,2,1,0:T(8,128)} async-done(((f32[3,24,64,64]{3,2,1,0:T(8,128)}), f32[3,24,64,64]{3,2,1,0:T(8,128)}) %all-reduce.2.cloned.1.call-update) | async-done | bytes 1179664 | tf_op jit(solution)/shard_map/psum | solution.py:139
  688.1 8.7 %fusion.43 = f32[64,3,24,64]{3,0,2,1:T(8,128)S(1)} fusion(f32[3,24,64,64]{3,2,1,0:T(8,128)} %all-reduce.2.cloned.1.call-done, f32[64]{0:T(128)S(1)} %iota_convert_fusion, f32[64]{0:T(128)S(1)} %get-tuple-element.267, f32[64]{0:T(128)S(1)} %get-tuple-element.266), kind=kOutput, calls=%fused_computation.64 | convolution fusion | flops 226504704 | bytes 2360064 | tf_op jit(solution)/shard_map/abil,lk->aibk/dot_general | solution.py:41
  696.7 2.2 fusion.35
  698.9 1.3 copy.131
  700.3 1.5 convert_element_type.76
  703.7 2.2 reshape.234
  707.3 2.2 reshape.236
  (168 shorter events, 43.1 us)
Async XLA Ops:
  7.2 263.4 %copy-start = (bf16[1,192,1536]{2,1,0:T(8,128)(2,1)S(1)}, bf16[1,192,1536]{2,1,0:T(8,128)(2,1)}, u32[]{:S(2)}) copy-start(bf16[1,192,1536]{2,1,0:T(8,128)(2,1)} %param.14) | copy-start | bytes 1769476
  9.6 31.4 %copy-start.8 = (bf16[1,128,2048]{2,1,0:T(8,128)(2,1)S(1)}, bf16[1,128,2048]{2,1,0:T(8,128)(2,1)}, u32[]{:S(2)}) copy-start(bf16[1,128,2048]{2,1,0:T(8,128)(2,1)} %param.13) | copy-start | bytes 1572868
  22.6 45.6 %all-to-all-start = ((bf16[16,2,8192]{2,1,0:T(2,128)(2,1)}), bf16[16,2,8192]{2,1,0:T(2,128)(2,1)S(1)}, u32[]{:S(2)}, u32[]{:S(2)}) async-start(bf16[16,2,8192]{2,1,0:T(2,128)(2,1)} %reshape.223), calls=%async_computation | async-start | bytes 1048576 | tf_op jit(solution)/shard_map/all_to_all | solution.py:124
  41.7 35.4 %copy-start.9 = (bf16[1,128,2048]{2,1,0:T(8,128)(2,1)S(1)}, bf16[1,128,2048]{2,1,0:T(8,128)(2,1)}, u32[]{:S(2)}) copy-start(bf16[1,128,2048]{2,1,0:T(8,128)(2,1)} %param.11) | copy-start | bytes 1572868
  68.1 29.3 %all-to-all-start.1 = ((bf16[16,2,8192]{2,1,0:T(2,128)(2,1)}), bf16[16,2,8192]{2,1,0:T(2,128)(2,1)S(1)}, u32[]{:S(2)}, u32[]{:S(2)}) async-start(bf16[16,2,8192]{2,1,0:T(2,128)(2,1)} %reshape.225), calls=%async_computation.1 | async-start | bytes 1048576 | tf_op jit(solution)/shard_map/all_to_all | solution.py:127
  97.5 24.1 %all-to-all-start.2 = ((bf16[16,2,8192]{2,1,0:T(2,128)(2,1)}), bf16[16,2,8192]{2,1,0:T(2,128)(2,1)S(1)}, u32[]{:S(2)}, u32[]{:S(2)}) async-start(bf16[16,2,8192]{2,1,0:T(2,128)(2,1)} %reshape.227), calls=%async_computation.2 | async-start | bytes 1048576 | tf_op jit(solution)/shard_map/all_to_all | solution.py:125
  121.6 31.1 %all-to-all-start.3 = ((bf16[16,2,8192]{2,1,0:T(2,128)(2,1)}), bf16[16,2,8192]{2,1,0:T(2,128)(2,1)}, u32[]{:S(2)}, u32[]{:S(2)}) async-start(bf16[16,2,8192]{2,1,0:T(2,128)(2,1)} %reshape.229), calls=%async_computation.3 | async-start | bytes 1048576 | tf_op jit(solution)/shard_map/all_to_all | solution.py:126
  161.5 1.0 copy-start.5
  164.5 2.4 copy-start.2
  167.0 1.2 copy-start.1
  167.0 1.3 copy-start.6
  167.4 2.3 copy-start.3
  169.7 0.7 copy-start.7
  172.4 1.0 copy-start.5
  175.4 2.6 copy-start.2
  178.0 1.2 copy-start.1
  178.0 1.3 copy-start.6
  178.3 2.3 copy-start.3
  180.7 0.7 copy-start.7
  181.4 3.7 copy-start.4
  181.4 4.0 copy-start.11
  185.4 0.8 copy-start.12
  191.7 1.0 copy-start.5
  194.7 2.4 copy-start.2
  197.2 1.2 copy-start.1
  197.2 1.3 copy-start.6
  197.5 2.3 copy-start.3
  199.9 0.7 copy-start.7
  202.6 1.0 copy-start.5
  205.6 2.6 copy-start.2
  208.1 1.2 copy-start.1
  208.1 1.3 copy-start.6
  208.5 2.3 copy-start.3
  210.8 0.7 copy-start.7
  211.5 3.7 copy-start.4
  211.5 4.0 copy-start.11
  215.6 0.8 copy-start.12
  218.2 16.3 %copy-start.10 = (bf16[2,1,1024,1,128]{4,2,0,3,1:T(8,128)(2,1)S(1)}, bf16[2,1,1024,1,128]{4,2,0,3,1:T(8,128)(2,1)}, u32[]{:S(2)}) copy-start(bf16[2,1,1024,1,128]{4,2,0,3,1:T(8,128)(2,1)} %get-tuple-element.93) | copy-start | bytes 1572868
  230.7 24.4 %all-to-all-start.4 = ((bf16[16,2,8192]{2,1,0:T(2,128)(2,1)}), bf16[16,2,8192]{2,1,0:T(2,128)(2,1)S(1)}, u32[]{:S(2)}, u32[]{:S(2)}) async-start(bf16[16,2,8192]{2,1,0:T(2,128)(2,1)} %reshape.231), calls=%async_computation.4 | async-start | bytes 1048576 | tf_op jit(solution)/shard_map/all_to_all | solution.py:131
  242.6 27.7 %copy-start.15 = (s32[3]{0:T(128)S(1)}, s32[3]{0:T(128)}, u32[]{:S(2)}) copy-start(s32[3]{0:T(128)} %constant.97) | copy-start | bytes 40
  242.6 27.8 %copy-start.14 = (s32[3]{0:T(128)S(1)}, s32[3]{0:T(128)}, u32[]{:S(2)}) copy-start(s32[3]{0:T(128)} %constant.100) | copy-start | bytes 40
  255.1 75.8 %all-to-all-start.5 = ((bf16[16,2,8192]{2,1,0:T(2,128)(2,1)}), bf16[16,2,8192]{2,1,0:T(2,128)(2,1)}, u32[]{:S(2)}, u32[]{:S(2)}) async-start(bf16[16,2,8192]{2,1,0:T(2,128)(2,1)} %reshape.233), calls=%async_computation.5 | async-start | bytes 1048576 | tf_op jit(solution)/shard_map/all_to_all | solution.py:132
  287.8 22.3 %copy-start.13 = (bf16[2,1,1024,1,128]{4,2,0,3,1:T(8,128)(2,1)S(1)}, bf16[2,1,1024,1,128]{4,2,0,3,1:T(8,128)(2,1)}, u32[]{:S(2)}) copy-start(bf16[2,1,1024,1,128]{4,2,0,3,1:T(8,128)(2,1)} %get-tuple-element.94) | copy-start | bytes 1572868
  330.8 376.4 %all-to-all-start.6 = ((bf16[16,2,8192]{2,1,0:T(2,128)(2,1)}), bf16[16,2,8192]{2,1,0:T(2,128)(2,1)}, u32[]{:S(2)}, u32[]{:S(2)}) async-start(bf16[16,2,8192]{2,1,0:T(2,128)(2,1)} %reshape.235), calls=%async_computation.6 | async-start | bytes 1048576 | tf_op jit(solution)/shard_map/all_to_all | solution.py:133
  344.9 343.2 %all-reduce.2.cloned.1.call-start = ((), (), s32[]{:S(2)}) async-start(), calls=%async_computation.7 | async-start | bytes 4718592 | tf_op jit(solution)/shard_map/psum | solution.py:139
Sparse Core Ops, SparseCore 0:
  363.4 324.6 all-reduce.1
where the time goes:
time: 728 us; the launch traced here: 718 us
  waiting for transfers between devices  359 us (49%)
  local copies, waits for them, and re-layouts  107 us (15%)
  other arithmetic  105 us (14%)
  starting transfers between devices  79.8 us (11%)
  matrix products  51.8 us (7%)
  between operations  14.7 us (2%)
    psum x1, waiting for transfers between devices, on_device(): total = lax.psum(spread(kept, own_index), 'replica')  325 us
    unnamed x11, other arithmetic  97.4 us
    unnamed x44, local copies, waits for them, and re-layouts  26.7 us
    gather x2, local copies, waits for them, and re-layouts, on_device(): kept = jnp.take_along_axis(coeffs, own_index, axis=-1)  22.3 us
    all_to_all x1, starting transfers between devices, on_device(): lax.all_to_all(query_rows, 'seq', split_axis=2, concat_axis=1, tiled=True)  18.4 us
  transfers between devices with their start and end apart: 8, of which 5 were waited for; matrix products, arithmetic and copies ran while one was open for 23% of the time, Pallas kernels for 0%

commit v1 on v0

v1 whole, which is shorter than its diff:
```python
import functools
import math

import jax
import jax.numpy as jnp
import numpy as np
from jax import lax
from jax.experimental import pallas as pl
from jax.experimental.pallas import tpu as pltpu
from jax.sharding import PartitionSpec as P

MESH = pl.DeviceIdType.MESH
HEAD = 128
GROUP = 64
NWIN = 8
TOK = 128
LEN = NWIN * TOK
QB = 256
ROWS = 192
COLS = 1536
LANES = 384
F32 = jnp.float32
BF16 = jnp.bfloat16
HIGH = lax.Precision.HIGHEST


def tables():
    i = np.arange(GROUP)[:, None].astype(np.float64)
    j = np.arange(GROUP)[None, :].astype(np.float64)
    c = np.where(i == 0, math.sqrt(1.0 / GROUP), math.sqrt(2.0 / GROUP)) * np.cos(
        math.pi * (2.0 * j + 1.0) * i / (2.0 * GROUP)
    )
    perm = np.concatenate([c[0::2], c[1::2]], axis=0)
    crow = np.kron(np.eye(3), perm)
    ccol = np.kron(np.eye(2), c)
    return crow.astype(np.float32), crow.T.astype(np.float32).copy(), ccol.astype(np.float32)


def kernel(
    q_ref, k_ref, v_ref, g_ref, drift_ref, idx_ref, crow_ref, crowt_ref, ccol_ref,
    dq_ref, dk_ref, dv_ref, outer_ref,
    inb, outb, kt_buf, dk_acc, dv_acc, drift_buf, idx_buf, crow, crowt, ccol, kept, vbuf, outer_buf,
    ss_in, rs_in, ss_out, rs_out, ss_kept, rs_kept, lsem,
):
    rep = lax.axis_index("replica")
    seq = lax.axis_index("seq")
    base = (seq // NWIN) * NWIN
    mine = seq % NWIN
    x = rep // 8
    zlo = (rep // 2) % 4
    core = rep % 2
    m = x * 2 + core
    ins = (q_ref, k_ref, v_ref, g_ref)
    outs = (dq_ref, dk_ref, dv_ref)

    def rep_z(k):
        return x * 8 + ((zlo + k) % 4) * 2 + core

    def rep_m(k):
        m2 = (m + k) % 8
        return (m2 // 2) * 8 + zlo * 2 + m2 % 2

    barrier = pltpu.get_barrier_semaphore()
    for k in range(1, NWIN):
        pl.semaphore_signal(barrier, inc=1, device_id={"seq": base + (mine + k) % NWIN}, device_id_type=MESH)
    for k in range(1, 4):
        pl.semaphore_signal(barrier, inc=1, device_id={"replica": rep_z(k)}, device_id_type=MESH)
    for k in range(1, 8):
        pl.semaphore_signal(barrier, inc=1, device_id={"replica": rep_m(k)}, device_id_type=MESH)

    locals_ = [
        pltpu.make_async_copy(drift_ref.at[0], drift_buf, lsem.at[0]),
        pltpu.make_async_copy(idx_ref.at[rep], idx_buf, lsem.at[1]),
        pltpu.make_async_copy(crow_ref, crow, lsem.at[2]),
        pltpu.make_async_copy(crowt_ref, crowt, lsem.at[3]),
        pltpu.make_async_copy(ccol_ref, ccol, lsem.at[4]),
    ]
    for c in locals_:
        c.start()
    my_rows = pl.ds(pl.multiple_of(mine * TOK, TOK), TOK)
    own = []
    for h in range(2):
        for a in range(4):
            c = pltpu.make_async_copy(
                ins[a].at[0, :, pl.ds(pl.multiple_of(mine * 256 + h * HEAD, HEAD), HEAD)],
                inb.at[h, a, my_rows, :],
                rs_in.at[h, a],
            )
            c.start()

    pl.semaphore_wait(barrier, 7 + 3 + 7)

    for h in range(2):
        for a in range(4):

            def send(s, carry, h=h, a=a):
                to = (mine + s) % NWIN
                pltpu.make_async_remote_copy(
                    src_ref=ins[a].at[0, :, pl.ds(pl.multiple_of(to * 256 + h * HEAD, HEAD), HEAD)],
                    dst_ref=inb.at[h, a, my_rows, :],
                    send_sem=ss_in.at[a],
                    recv_sem=rs_in.at[h, a],
                    device_id={"seq": base + to},
                    device_id_type=MESH,
                ).start()
                return carry

            lax.fori_loop(1, NWIN, send, 0)

    for c in locals_:
        c.wait()
    lane = lax.broadcasted_iota(jnp.int32, (1, LANES), 1)
    tile32 = jnp.where(
        lax.broadcasted_iota(jnp.int32, (32, LANES), 0) == lax.broadcasted_iota(jnp.int32, (32, LANES), 1) % 32,
        1.0,
        0.0,
    ).astype(BF16)
    off = jnp.zeros((12, LANES), F32)
    slot_base = lax.broadcasted_iota(jnp.int32, (12, 32), 1) * 128
    for bm in range(2):
        for a in range(3):
            o = (idx_buf[a, bm * 12 : bm * 12 + 12, :] - slot_base).astype(F32).astype(BF16)
            tiled = jnp.dot(o, tile32, preferred_element_type=F32)
            off = jnp.where(lane // 64 == bm * 3 + a, tiled, off)
    off = off - ((lane // 32) % 2 * GROUP).astype(F32)
    kept[m, zlo, 0] = jnp.zeros((16, LANES), F32)
    kept[m, zlo, 1] = jnp.zeros((16, LANES), F32)
    kept[m, zlo, 1, 0:12, :] = off
    sub = lax.broadcasted_iota(jnp.int32, (GROUP, LANES), 0).astype(F32)

    def forward(t, carry):
        at = pl.multiple_of(t * 128, 128)
        pieces = []
        for bm in range(2):
            xt = drift_buf[:, pl.ds(at + bm * 768, 128)].astype(F32)
            pieces.append(jnp.dot(crow[...], xt, precision=HIGH, preferred_element_type=F32))
        y = jnp.concatenate(pieces, axis=0)
        u = lax.dot_general(ccol[...], y, (((1,), (1,)), ((), ())), precision=HIGH, preferred_element_type=F32)
        for bl in range(2):
            row = kept[m, zlo, 1, pl.ds(t * 2 + bl, 1), :]
            hit = jnp.where(sub == row, u[bl * GROUP : (bl + 1) * GROUP, :], 0.0)
            kept[m, zlo, 0, pl.ds(t * 2 + bl, 1), :] = jnp.sum(hit, axis=0, keepdims=True)
        return carry

    lax.fori_loop(0, 6, forward, 0)
    for k in range(1, 4):
        pltpu.make_async_remote_copy(
            src_ref=kept.at[m, zlo],
            dst_ref=kept.at[m, zlo],
            send_sem=ss_kept.at[0],
            recv_sem=rs_kept.at[0],
            device_id={"replica": rep_z(k)},
            device_id_type=MESH,
        ).start()

    scale = 1.0 / math.sqrt(HEAD)
    my_cols = lambda h: pl.ds(pl.multiple_of(mine * 256 + h * HEAD, HEAD), HEAD)

    def give(h, a, i):
        rows = pl.ds(pl.multiple_of(i * TOK, TOK), TOK)

        @pl.when(i == mine)
        def _():
            pltpu.make_async_copy(outb.at[h, a, rows, :], outs[a].at[0, :, my_cols(h)], rs_out.at[a]).start()

        @pl.when(i != mine)
        def _():
            pltpu.make_async_remote_copy(
                src_ref=outb.at[h, a, rows, :],
                dst_ref=outs[a].at[0, :, my_cols(h)],
                send_sem=ss_out.at[a],
                recv_sem=rs_out.at[a],
                device_id={"seq": base + i},
                device_id_type=MESH,
            ).start()

    def attend(h):
        for a in range(4):
            pltpu.make_async_copy(inb.at[h, a], inb.at[h, a], rs_in.at[h, a]).wait()
        kt_buf[...] = jnp.transpose(inb[h, 1].astype(F32)).astype(BF16)
        dk_acc[...] = jnp.zeros_like(dk_acc)
        dv_acc[...] = jnp.zeros_like(dv_acc)

        def step(b, carry):
            rows = pl.ds(pl.multiple_of(b * QB, QB), QB)
            qb = inb[h, 0, rows, :]
            gb = inb[h, 3, rows, :]
            nt = (((1,), (1,)), ((), ()))
            s = lax.dot_general(inb[h, 1], qb, nt, preferred_element_type=F32)
            top = jnp.max(s, axis=0, keepdims=True)
            e = jnp.exp((s - top) * scale)
            p = e * (1.0 / jnp.sum(e, axis=0, keepdims=True))
            low = p.astype(BF16)
            d = lax.dot_general(inb[h, 2], gb, nt, preferred_element_type=F32)
            delta = jnp.sum(low.astype(F32) * d, axis=0, keepdims=True)
            sg = (p * (d - delta)).astype(BF16)
            dqt = jnp.dot(kt_buf[...], sg, preferred_element_type=F32) * scale
            outb[h, 0, rows, :] = jnp.transpose(dqt).astype(BF16)
            dv_acc[...] += jnp.dot(low, gb, preferred_element_type=F32)
            dk_acc[...] += jnp.dot(sg, qb, preferred_element_type=F32)
            for u in range(QB // TOK):
                give(h, 0, b * (QB // TOK) + u)
            return carry

        lax.fori_loop(0, LEN // QB, step, 0)
        outb[h, 1] = (dk_acc[...] * scale).astype(BF16)
        outb[h, 2] = dv_acc[...].astype(BF16)

        def rest(i, carry):
            give(h, 1, i)
            give(h, 2, i)
            return carry

        lax.fori_loop(0, NWIN, rest, 0)

    attend(0)

    pltpu.make_async_copy(kept.at[m, 0:3], kept.at[m, 0:3], rs_kept.at[0]).wait()
    for k in range(1, 8):
        pltpu.make_async_remote_copy(
            src_ref=kept.at[m],
            dst_ref=kept.at[m],
            send_sem=ss_kept.at[1],
            recv_sem=rs_kept.at[1],
            device_id={"replica": rep_m(k)},
            device_id_type=MESH,
        ).start()

    attend(1)

    pltpu.make_async_copy(kept.at[0:7], kept.at[0:7], rs_kept.at[1]).wait()

    def backward(t, carry):
        at = pl.multiple_of(t * 128, 128)
        zs = []
        for bl in range(2):

            def add(r, z):
                one = pl.ds(t * 2 + bl, 1)
                for s in range(4):
                    z = z + jnp.where(sub == kept[r, s, 1, one, :], kept[r, s, 0, one, :], 0.0)
                return z

            zs.append(lax.fori_loop(0, 8, add, jnp.zeros((GROUP, LANES), F32)))
        z = jnp.transpose(jnp.concatenate(zs, axis=0))
        w = jnp.dot(z, ccol[...], precision=HIGH, preferred_element_type=F32)
        for bm in range(2):
            o = jnp.dot(crowt[...], w[bm * ROWS : (bm + 1) * ROWS, :], precision=HIGH, preferred_element_type=F32)
            outer_buf[:, pl.ds(at + bm * 768, 128)] = o.astype(BF16)
        return carry

    lax.fori_loop(0, 6, backward, 0)
    last = pltpu.make_async_copy(outer_buf, outer_ref, lsem.at[5])
    last.start()

    part = pl.ds(0, 14 * HEAD)
    for a in range(4):
        pltpu.make_async_copy(ins[a].at[0, :, part], ins[a].at[0, :, part], ss_in.at[a]).wait()
    pltpu.make_async_copy(kept.at[0, 0:3], kept.at[0, 0:3], ss_kept.at[0]).wait()
    pltpu.make_async_copy(kept.at[0:7], kept.at[0:7], ss_kept.at[1]).wait()
    for a in range(3):
        pltpu.make_async_copy(outs[a].at[0, :, part], outs[a].at[0, :, part], ss_out.at[a]).wait()
    for a in range(3):
        pltpu.make_async_copy(outs[a].at[0], outs[a].at[0], rs_out.at[a]).wait()
    last.wait()


def on_device(query_rows, key_rows, value_rows, out_grad, drift, kept_index):
    crow, crowt, ccol = (jnp.asarray(t) for t in tables())
    anyspec = pl.BlockSpec(memory_space=pl.ANY)
    rows = jax.ShapeDtypeStruct((1, TOK, 2048), BF16)
    return pl.pallas_call(
        kernel,
        out_shape=(rows, rows, rows, jax.ShapeDtypeStruct((ROWS, COLS), BF16)),
        in_specs=[anyspec] * 9,
        out_specs=[anyspec] * 4,
        scratch_shapes=[
            pltpu.VMEM((2, 4, LEN, HEAD), BF16),
            pltpu.VMEM((2, 3, LEN, HEAD), BF16),
            pltpu.VMEM((HEAD, LEN), BF16),
            pltpu.VMEM((LEN, HEAD), F32),
            pltpu.VMEM((LEN, HEAD), F32),
            pltpu.VMEM((ROWS, COLS), BF16),
            pltpu.VMEM((3, 24, 32), jnp.int32),
            pltpu.VMEM((ROWS, ROWS), F32),
            pltpu.VMEM((ROWS, ROWS), F32),
            pltpu.VMEM((128, 128), F32),
            pltpu.VMEM((8, 4, 2, 16, LANES), F32),
            pltpu.VMEM((8, 128), F32),
            pltpu.VMEM((ROWS, COLS), BF16),
            pltpu.SemaphoreType.DMA((4,)),
            pltpu.SemaphoreType.DMA((2, 4)),
            pltpu.SemaphoreType.DMA((3,)),
            pltpu.SemaphoreType.DMA((3,)),
            pltpu.SemaphoreType.DMA((2,)),
            pltpu.SemaphoreType.DMA((2,)),
            pltpu.SemaphoreType.DMA((6,)),
        ],
        compiler_params=pltpu.CompilerParams(
            collective_id=0, has_side_effects=True, vmem_limit_bytes=48 << 20
        ),
    )(query_rows, key_rows, value_rows, out_grad, drift, kept_index, crow, crowt, ccol)


def solution(mesh):
    tokens = P("replica", "seq", None)
    return jax.shard_map(
        on_device,
        mesh=mesh,
        in_specs=(tokens, tokens, tokens, tokens, tokens, P(None, "seq", None, None)),
        out_specs=(tokens, tokens, tokens, P("seq", None)),
        check_vma=False,
    )
```

time: 728 us -> 203 us (0.28)
  the two profiles are of different devices: /device:TPU:1 before, /device:TPU:105 now
where the time goes in v1:
time: 203 us; the launch traced here: 202 us
  Pallas kernels  191 us (94%)
  local copies, waits for them, and re-layouts  11.1 us (5%)
    pallas_call x1, Pallas kernels, on_device(): pl.pallas_call(kernel, out_shape=(rows, rows, rows, jax.ShapeDtypeStruct(...  191 us
    unnamed x20, local copies, waits for them, and re-layouts  11.1 us

profile of v1, /device:TPU:105, one launch (start us, length us, event | category | flops | bytes accessed | tf_op | source)
XLA Modules:
  0.0 202.3 jit_solution(13876746639507784187)
XLA Ops:
  0.6 0.0 copy-start
  0.6 1.1 copy-done
  1.7 0.0 copy-start.1
  1.7 1.0 copy-done.1
  2.7 0.0 copy-start.2
  2.7 1.0 copy-done.2
  3.8 0.0 copy-start.3
  3.8 1.0 copy-done.3
  4.8 0.0 copy-start.4
  4.8 1.0 copy-done.4
  5.9 0.0 copy-start.5
  5.9 0.9 copy-done.5
  6.8 0.0 copy-start.6
  6.8 0.9 copy-done.6
  7.7 0.0 copy-start.7
  7.7 0.8 copy-done.7
  8.6 190.6 %shard_map.120 = (bf16[1,128,2048]{2,1,0:T(8,128)(2,1)S(1)}, bf16[1,128,2048]{2,1,0:T(8,128)(2,1)S(1)}, bf16[1,128,2048]{2,1,0:T(8,128)(2,1)S(1)}, bf16[192,1536]{1,0:T(8,128)(2,1)S(1)}) custom-call(bf16[1,128,2048]{2,1,0:T(8,128)(2,1)S(1)} %copy-done.1, bf16[1,128,2048]{2,1,0:T(8,128)(2,1)S(1)} %copy-done.2, bf16[1,128,2048]{2,1,0:T(8,128)(2,1)S(1)} %copy-done.3, ...), custom_call_target="tpu_custom_call" | custom-call | tf_op jit(solution)/shard_map/pallas_call | solution.py:272
  199.1 0.8 copy.17
  199.9 0.8 copy.18
  200.7 0.8 copy.19
  201.5 0.8 copy.20
Async XLA Ops:
  0.6 1.1 copy-start
  1.7 1.0 copy-start.1
  2.7 1.0 copy-start.2
  3.8 1.0 copy-start.3
  4.8 1.0 copy-start.4
  5.9 0.9 copy-start.5
  6.8 0.9 copy-start.6
  7.7 0.8 copy-start.7

commit v2 on v1

v2 whole, which is shorter than its diff:
```python
import functools
import math

import jax
import jax.numpy as jnp
import numpy as np
from jax import lax
from jax.experimental import pallas as pl
from jax.experimental.pallas import tpu as pltpu
from jax.sharding import PartitionSpec as P

MESH = pl.DeviceIdType.MESH
HEAD = 128
GROUP = 64
NWIN = 8
TOK = 128
LEN = NWIN * TOK
WIDE = 2 * HEAD
QB = 256
ROWS = 192
COLS = 1536
LANES = 384
F32 = jnp.float32
BF16 = jnp.bfloat16
HIGH = lax.Precision.HIGHEST


def tables():
    i = np.arange(GROUP)[:, None].astype(np.float64)
    j = np.arange(GROUP)[None, :].astype(np.float64)
    c = np.where(i == 0, math.sqrt(1.0 / GROUP), math.sqrt(2.0 / GROUP)) * np.cos(
        math.pi * (2.0 * j + 1.0) * i / (2.0 * GROUP)
    )
    perm = np.concatenate([c[0::2], c[1::2]], axis=0)
    crow = np.kron(np.eye(3), perm)
    ccol = np.kron(np.eye(2), c)
    return crow.astype(np.float32), crow.T.astype(np.float32).copy(), ccol.astype(np.float32)


def kernel(
    q_ref, k_ref, v_ref, g_ref, drift_ref, idx_ref, crow_ref, crowt_ref, ccol_ref,
    dq_ref, dk_ref, dv_ref, outer_ref,
    inb, outb, kt_buf, dk_acc, dv_acc, drift_buf, idx_buf, crow, crowt, ccol, kept, picked, place, wide, outer_buf,
    ss_in, rs_kv, rs_q, rs_g, ss_out, rs_out, ss_kept, rs_kept, lsem,
):
    rep = lax.axis_index("replica")
    seq = lax.axis_index("seq")
    base = (seq // NWIN) * NWIN
    mine = seq % NWIN
    pair = mine // 2
    x = rep // 8
    zlo = (rep // 2) % 4
    core = rep % 2
    m = x * 2 + core
    ins = (q_ref, k_ref, v_ref, g_ref)
    outs = (dq_ref, dk_ref, dv_ref)

    def rep_z(k):
        return x * 8 + ((zlo + k) % 4) * 2 + core

    def rep_m(k):
        m2 = (m + k) % 8
        return (m2 // 2) * 8 + zlo * 2 + m2 % 2

    def rows_of(i):
        return pl.ds(pl.multiple_of(i * TOK, TOK), TOK)

    def cols_of(i):
        return pl.ds(pl.multiple_of(i * WIDE, WIDE), WIDE)

    barrier = pltpu.get_barrier_semaphore()
    for k in range(1, NWIN):
        pl.semaphore_signal(barrier, inc=1, device_id={"seq": base + (mine + k) % NWIN}, device_id_type=MESH)
    for k in range(1, 4):
        pl.semaphore_signal(barrier, inc=1, device_id={"replica": rep_z(k)}, device_id_type=MESH)
    for k in range(1, 8):
        pl.semaphore_signal(barrier, inc=1, device_id={"replica": rep_m(k)}, device_id_type=MESH)

    locals_ = [
        pltpu.make_async_copy(drift_ref.at[0], drift_buf, lsem.at[0]),
        pltpu.make_async_copy(idx_ref, idx_buf, lsem.at[1]),
        pltpu.make_async_copy(crow_ref, crow, lsem.at[2]),
        pltpu.make_async_copy(crowt_ref, crowt, lsem.at[3]),
        pltpu.make_async_copy(ccol_ref, ccol, lsem.at[4]),
    ]
    for c in locals_:
        c.start()

    def arrival(a):
        return (rs_q.at[mine], rs_kv.at[0], rs_kv.at[1], rs_g.at[mine])[a]

    for a in range(4):
        pltpu.make_async_copy(ins[a].at[0, :, cols_of(mine)], inb.at[a, rows_of(mine), :], arrival(a)).start()

    pl.semaphore_wait(barrier, 7 + 3 + 7)

    def send(a, to):
        pltpu.make_async_remote_copy(
            src_ref=ins[a].at[0, :, cols_of(to)],
            dst_ref=inb.at[a, rows_of(mine), :],
            send_sem=ss_in.at[a],
            recv_sem=arrival(a),
            device_id={"seq": base + to},
            device_id_type=MESH,
        ).start()

    mate = pair * 2 + 1 - mine % 2

    def others(group):
        for a in group:
            send(a, mate)

        def more(n, carry):
            to = ((pair + 4 - n // 2) % 4) * 2 + n % 2
            for a in group:
                send(a, to)
            return carry

        lax.fori_loop(2, NWIN, more, 0)

    others((1, 2))
    others((0, 3))

    for c in locals_:
        c.wait()
    lane = lax.broadcasted_iota(jnp.int32, (1, LANES), 1)
    parity = ((lane // 32) % 2 * GROUP).astype(F32)
    first_half = lane < ROWS
    slot_base = lax.broadcasted_iota(jnp.int32, (32 * 24, 32), 1) * 128
    jrow = lax.broadcasted_iota(jnp.int32, (32, LANES), 0)
    jlane = lax.broadcasted_iota(jnp.int32, (32, LANES), 1)
    spots = jnp.zeros((32 * 24, LANES), F32) - parity
    for a in range(3):
        o = (idx_buf[:, a].reshape(32 * 24, 32) - slot_base).astype(F32).astype(BF16)
        at_a = jnp.where((jrow == jlane % 32) & ((jlane // 64) % 3 == a), 1.0, 0.0).astype(BF16)
        spots = spots + jnp.dot(o, at_a, preferred_element_type=F32)
    place[...] = spots.reshape(32, 24, LANES)
    sub = lax.broadcasted_iota(jnp.int32, (GROUP, LANES), 0).astype(F32)

    def halves(ref, r, row):
        return jnp.where(first_half, ref[r, pl.ds(row, 1), :], ref[r, pl.ds(row + 12, 1), :])

    def forward(t, carry):
        at = pl.multiple_of(t * 128, 128)
        pieces = []
        for bm in range(2):
            xt = drift_buf[:, pl.ds(at + bm * 768, 128)].astype(F32)
            pieces.append(jnp.dot(crow[...], xt, precision=HIGH, preferred_element_type=F32))
        y = jnp.concatenate(pieces, axis=0)
        u = lax.dot_general(ccol[...], y, (((1,), (1,)), ((), ())), precision=HIGH, preferred_element_type=F32)
        for bl in range(2):
            hit = jnp.where(sub == halves(place, rep, t * 2 + bl), u[bl * GROUP : (bl + 1) * GROUP, :], 0.0)
            picked[pl.ds(t * 2 + bl, 1), :] = jnp.sum(hit, axis=0, keepdims=True)
        return carry

    lax.fori_loop(0, 6, forward, 0)
    wl = lax.broadcasted_iota(jnp.int32, (LANES, 128), 0)
    nl = lax.broadcasted_iota(jnp.int32, (LANES, 128), 1)
    same = ((wl // 64) % 3 == nl // 32) & (wl % 32 == nl % 32)
    for bm in range(2):
        gather = jnp.where(same & (wl // ROWS == bm), 1.0, 0.0)
        kept[m, zlo, bm * 12 : bm * 12 + 12, :] = jnp.dot(
            picked[0:12, :], gather, precision=HIGH, preferred_element_type=F32
        )
    for k in range(1, 4):
        pltpu.make_async_remote_copy(
            src_ref=kept.at[m, zlo],
            dst_ref=kept.at[m, zlo],
            send_sem=ss_kept.at[0],
            recv_sem=rs_kept.at[0],
            device_id={"replica": rep_z(k)},
            device_id_type=MESH,
        ).start()

    scale = 1.0 / math.sqrt(HEAD)
    nt = (((1,), (1,)), ((), ()))

    def give(a, i):
        @pl.when(i == mine)
        def _():
            pltpu.make_async_copy(outb.at[a, rows_of(i), :], outs[a].at[0, :, cols_of(mine)], rs_out.at[a]).start()

        @pl.when(i != mine)
        def _():
            pltpu.make_async_remote_copy(
                src_ref=outb.at[a, rows_of(i), :],
                dst_ref=outs[a].at[0, :, cols_of(mine)],
                send_sem=ss_out.at[a],
                recv_sem=rs_out.at[a],
                device_id={"seq": base + i},
                device_id_type=MESH,
            ).start()

    for a in (1, 2):
        pltpu.make_async_copy(inb.at[a], inb.at[a], rs_kv.at[a - 1]).wait()
    for h in range(2):
        of_head = slice(h * HEAD, (h + 1) * HEAD)
        kt_buf[h] = jnp.transpose(inb[1, :, of_head].astype(F32)).astype(BF16)
    dk_acc[...] = jnp.zeros_like(dk_acc)
    dv_acc[...] = jnp.zeros_like(dv_acc)

    pltpu.make_async_copy(kept.at[m, 0:3], kept.at[m, 0:3], rs_kept.at[0]).wait()
    for k in range(1, 8):
        pltpu.make_async_remote_copy(
            src_ref=kept.at[m],
            dst_ref=kept.at[m],
            send_sem=ss_kept.at[1],
            recv_sem=rs_kept.at[1],
            device_id={"replica": rep_m(k)},
            device_id_type=MESH,
        ).start()

    def step(n, carry):
        b = (pair + n) % 4
        for u in range(2):
            i = b * 2 + u
            pltpu.make_async_copy(inb.at[0, rows_of(i)], inb.at[0, rows_of(i)], rs_q.at[i]).wait()
            pltpu.make_async_copy(inb.at[3, rows_of(i)], inb.at[3, rows_of(i)], rs_g.at[i]).wait()
        rows = pl.ds(pl.multiple_of(b * QB, QB), QB)
        for h in range(2):
            of_head = slice(h * HEAD, (h + 1) * HEAD)
            qb = inb[0, rows, of_head]
            gb = inb[3, rows, of_head]
            s = lax.dot_general(inb[1, :, of_head], qb, nt, preferred_element_type=F32)
            top = jnp.max(s, axis=0, keepdims=True)
            e = jnp.exp((s - top) * scale)
            p = e * (1.0 / jnp.sum(e, axis=0, keepdims=True))
            low = p.astype(BF16)
            d = lax.dot_general(inb[2, :, of_head], gb, nt, preferred_element_type=F32)
            delta = jnp.sum(low.astype(F32) * d, axis=0, keepdims=True)
            sg = (p * (d - delta)).astype(BF16)
            dqt = jnp.dot(kt_buf[h], sg, preferred_element_type=F32) * scale
            outb[0, rows, of_head] = jnp.transpose(dqt).astype(BF16)
            dv_acc[h] += jnp.dot(low, gb, preferred_element_type=F32)
            dk_acc[h] += jnp.dot(sg, qb, preferred_element_type=F32)
        for u in range(2):
            give(0, b * 2 + u)
        return carry

    lax.fori_loop(0, LEN // QB, step, 0)
    for h in range(2):
        of_head = slice(h * HEAD, (h + 1) * HEAD)
        outb[1, :, of_head] = (dk_acc[h] * scale).astype(BF16)
        outb[2, :, of_head] = dv_acc[h].astype(BF16)

    def rest(n, carry):
        i = ((pair + n // 2) % 4) * 2 + n % 2
        give(1, i)
        give(2, i)
        return carry

    lax.fori_loop(0, NWIN, rest, 0)

    pltpu.make_async_copy(kept.at[0:7], kept.at[0:7], rs_kept.at[1]).wait()
    nr = lax.broadcasted_iota(jnp.int32, (128, LANES), 0)
    wr = lax.broadcasted_iota(jnp.int32, (128, LANES), 1)
    widen = jnp.where(((wr // 64) % 3 == nr // 32) & (wr % 32 == nr % 32), 1.0, 0.0)

    def spread_out(i, carry):
        some = kept[i].reshape(4 * 24, 128)
        wide[pl.ds(i * 4, 4)] = jnp.dot(some, widen, precision=HIGH, preferred_element_type=F32).reshape(4, 24, LANES)
        return carry

    lax.fori_loop(0, 8, spread_out, 0)

    def backward(t, carry):
        at = pl.multiple_of(t * 128, 128)
        zs = []
        for bl in range(2):

            def add(i, z):
                for r in range(8):
                    slot = i * 8 + (r % 2) * 4 + r // 2
                    hit = sub == halves(place, i * 8 + r, t * 2 + bl)
                    z = z + jnp.where(hit, halves(wide, slot, t * 2 + bl), 0.0)
                return z

            zs.append(lax.fori_loop(0, 4, add, jnp.zeros((GROUP, LANES), F32)))
        z = jnp.transpose(jnp.concatenate(zs, axis=0))
        w = jnp.dot(z, ccol[...], precision=HIGH, preferred_element_type=F32)
        for bm in range(2):
            o = jnp.dot(crowt[...], w[bm * ROWS : (bm + 1) * ROWS, :], precision=HIGH, preferred_element_type=F32)
            outer_buf[:, pl.ds(at + bm * 768, 128)] = o.astype(BF16)
        return carry

    lax.fori_loop(0, 6, backward, 0)
    last = pltpu.make_async_copy(outer_buf, outer_ref, lsem.at[5])
    last.start()

    part = pl.ds(0, 7 * WIDE)
    for a in range(4):
        pltpu.make_async_copy(ins[a].at[0, :, part], ins[a].at[0, :, part], ss_in.at[a]).wait()
    pltpu.make_async_copy(kept.at[0, 0:3], kept.at[0, 0:3], ss_kept.at[0]).wait()
    pltpu.make_async_copy(kept.at[0:7], kept.at[0:7], ss_kept.at[1]).wait()
    for a in range(3):
        pltpu.make_async_copy(outs[a].at[0, :, part], outs[a].at[0, :, part], ss_out.at[a]).wait()
    for a in range(3):
        pltpu.make_async_copy(outs[a].at[0], outs[a].at[0], rs_out.at[a]).wait()
    last.wait()


def on_device(query_rows, key_rows, value_rows, out_grad, drift, kept_index):
    crow, crowt, ccol = (jnp.asarray(t) for t in tables())
    anyspec = pl.BlockSpec(memory_space=pl.ANY)
    rows = jax.ShapeDtypeStruct((1, TOK, 2048), BF16)
    return pl.pallas_call(
        kernel,
        out_shape=(rows, rows, rows, jax.ShapeDtypeStruct((ROWS, COLS), BF16)),
        in_specs=[anyspec] * 9,
        out_specs=[anyspec] * 4,
        scratch_shapes=[
            pltpu.VMEM((4, LEN, WIDE), BF16),
            pltpu.VMEM((3, LEN, WIDE), BF16),
            pltpu.VMEM((2, HEAD, LEN), BF16),
            pltpu.VMEM((2, LEN, HEAD), F32),
            pltpu.VMEM((2, LEN, HEAD), F32),
            pltpu.VMEM((ROWS, COLS), BF16),
            pltpu.VMEM((32, 3, 24, 32), jnp.int32),
            pltpu.VMEM((ROWS, ROWS), F32),
            pltpu.VMEM((ROWS, ROWS), F32),
            pltpu.VMEM((128, 128), F32),
            pltpu.VMEM((8, 4, 24, 128), F32),
            pltpu.VMEM((16, LANES), F32),
            pltpu.VMEM((32, 24, LANES), F32),
            pltpu.VMEM((32, 24, LANES), F32),
            pltpu.VMEM((ROWS, COLS), BF16),
            pltpu.SemaphoreType.DMA((4,)),
            pltpu.SemaphoreType.DMA((2,)),
            pltpu.SemaphoreType.DMA((NWIN,)),
            pltpu.SemaphoreType.DMA((NWIN,)),
            pltpu.SemaphoreType.DMA((3,)),
            pltpu.SemaphoreType.DMA((3,)),
            pltpu.SemaphoreType.DMA((2,)),
            pltpu.SemaphoreType.DMA((2,)),
            pltpu.SemaphoreType.DMA((6,)),
        ],
        compiler_params=pltpu.CompilerParams(
            collective_id=0, has_side_effects=True, vmem_limit_bytes=63 << 20
        ),
    )(query_rows, key_rows, value_rows, out_grad, drift, kept_index, crow, crowt, ccol)


def solution(mesh):
    tokens = P("replica", "seq", None)
    return jax.shard_map(
        on_device,
        mesh=mesh,
        in_specs=(tokens, tokens, tokens, tokens, tokens, P(None, "seq", None, None)),
        out_specs=(tokens, tokens, tokens, P("seq", None)),
        check_vma=False,
    )
```

time: 203 us -> 184 us (0.906)
  the two profiles are of different devices: /device:TPU:105 before, /device:TPU:1 now
where the time goes in v2:
time: 184 us
  Pallas kernels  179 us (97%)
  local copies, waits for them, and re-layouts  4.38 us (2%)
    pallas_call x1, Pallas kernels, on_device(): pl.pallas_call(kernel, out_shape=(rows, rows, rows, jax.ShapeDtypeStruct(...  179 us
    unnamed x10, local copies, waits for them, and re-layouts  4.38 us

profile of v2, /device:TPU:1, one launch (start us, length us, event | category | flops | bytes accessed | tf_op | source)
XLA Modules:
  0.0 184.2 jit_solution(7990950239516930920)
XLA Ops:
  0.6 179.1 %shard_map.120 = (bf16[1,128,2048]{2,1,0:T(8,128)(2,1)}, bf16[1,128,2048]{2,1,0:T(8,128)(2,1)}, bf16[1,128,2048]{2,1,0:T(8,128)(2,1)}, bf16[192,1536]{1,0:T(8,128)(2,1)}) custom-call(bf16[1,128,2048]{2,1,0:T(8,128)(2,1)} %q_ref.1, bf16[1,128,2048]{2,1,0:T(8,128)(2,1)} %k_ref.1, bf16[1,128,2048]{2,1,0:T(8,128)(2,1)} %v_ref.1, bf16[1,128,2048]{2,1,0:T(8,128)(2,1)} %g_ref.1, ...), custom_call_target="tpu_custom_call" | custom-call | tf_op jit(solution)/shard_map/pallas_call | solution.py:306
  179.8 0.0 copy-start.2
  179.8 0.0 copy-start.1
  179.8 2.0 %copy.17 = bf16[1,128,2048]{2,1,0:T(8,128)(2,1)} copy(bf16[1,128,2048]{2,1,0:T(8,128)(2,1)} %get-tuple-element.8) | data formatting | bytes 1048576
  181.8 0.0 copy-done.2
  181.8 0.0 copy-start
  181.8 0.8 copy.18
  182.6 0.0 copy-done.1
  182.6 0.8 copy.19
  183.4 0.0 copy-done
  183.4 0.8 copy.20
Async XLA Ops:
  179.8 2.0 %copy-start.2 = (bf16[1,128,2048]{2,1,0:T(8,128)(2,1)S(1)}, bf16[1,128,2048]{2,1,0:T(8,128)(2,1)}, u32[]{:S(2)}) copy-start(bf16[1,128,2048]{2,1,0:T(8,128)(2,1)} %get-tuple-element.9) | copy-start | bytes 1572868
  179.8 2.8 %copy-start.1 = (bf16[1,128,2048]{2,1,0:T(8,128)(2,1)S(1)}, bf16[1,128,2048]{2,1,0:T(8,128)(2,1)}, u32[]{:S(2)}) copy-start(bf16[1,128,2048]{2,1,0:T(8,128)(2,1)} %get-tuple-element.10) | copy-start | bytes 1572868
  181.8 1.6 copy-start

commit v3 on v2

--- a/solution.py
+++ b/solution.py
@@ -299,13 +299,27 @@
     last.wait()
 
 
+def place_results(*refs):
+    arrived, left = refs[12:]
+    into = [pltpu.make_async_copy(refs[i], refs[8 + i], arrived.at[i]) for i in range(4)]
+    out = [pltpu.make_async_copy(refs[8 + i], refs[4 + i], left.at[i]) for i in range(4)]
+    for c in into:
+        c.start()
+    for i in range(4):
+        into[i].wait()
+        out[i].start()
+    for c in out:
+        c.wait()
+
+
 def on_device(query_rows, key_rows, value_rows, out_grad, drift, kept_index):
     crow, crowt, ccol = (jnp.asarray(t) for t in tables())
     anyspec = pl.BlockSpec(memory_space=pl.ANY)
     rows = jax.ShapeDtypeStruct((1, TOK, 2048), BF16)
-    return pl.pallas_call(
+    results = (rows, rows, rows, jax.ShapeDtypeStruct((ROWS, COLS), BF16))
+    landed = pl.pallas_call(
         kernel,
-        out_shape=(rows, rows, rows, jax.ShapeDtypeStruct((ROWS, COLS), BF16)),
+        out_shape=results,
         in_specs=[anyspec] * 9,
         out_specs=[anyspec] * 4,
         scratch_shapes=[
@@ -338,6 +352,15 @@
             collective_id=0, has_side_effects=True, vmem_limit_bytes=63 << 20
         ),
     )(query_rows, key_rows, value_rows, out_grad, drift, kept_index, crow, crowt, ccol)
+    return pl.pallas_call(
+        place_results,
+        out_shape=results,
+        in_specs=[anyspec] * 4,
+        out_specs=[anyspec] * 4,
+        scratch_shapes=[pltpu.VMEM(r.shape, r.dtype) for r in results]
+        + [pltpu.SemaphoreType.DMA((4,)), pltpu.SemaphoreType.DMA((4,))],
+        compiler_params=pltpu.CompilerParams(vmem_limit_bytes=63 << 20),
+    )(*landed)
 
 
 def solution(mesh):

time: 184 us -> 182 us (0.989)
  local copies, waits for them, and re-layouts: 4.38 us -> 0 us
  Pallas kernels: 179 us -> 182 us
    unnamed x10 -> x0, local copies, waits for them, and re-layouts: 4.38 us -> none
    pallas_call x1 -> x2, Pallas kernels: 179 us -> 182 us  [the longest x1 179 us: on_device(): pl.pallas_call(kernel, out_shape=results, in_specs=[anyspec] * 9, out_spe...]
where the time goes in v3:
time: 182 us
  Pallas kernels  182 us (100%)
    pallas_call x1, Pallas kernels, on_device(): pl.pallas_call(kernel, out_shape=results, in_specs=[anyspec] * 9, out_spe...  179 us

profile of v3, /device:TPU:1, one launch (start us, length us, event | category | flops | bytes accessed | tf_op | source)
XLA Modules:
  0.0 182.2 jit_solution(14687083523578703553)
XLA Ops:
  0.6 179.1 %shard_map.120 = (bf16[1,128,2048]{2,1,0:T(8,128)(2,1)}, bf16[1,128,2048]{2,1,0:T(8,128)(2,1)}, bf16[1,128,2048]{2,1,0:T(8,128)(2,1)}, bf16[192,1536]{1,0:T(8,128)(2,1)}) custom-call(bf16[1,128,2048]{2,1,0:T(8,128)(2,1)} %q_ref.1, bf16[1,128,2048]{2,1,0:T(8,128)(2,1)} %k_ref.1, bf16[1,128,2048]{2,1,0:T(8,128)(2,1)} %v_ref.1, bf16[1,128,2048]{2,1,0:T(8,128)(2,1)} %g_ref.1, ...), custom_call_target="tpu_custom_call" | custom-call | tf_op jit(solution)/shard_map/pallas_call | solution.py:320
  179.8 2.4 %shard_map.121 = (bf16[1,128,2048]{2,1,0:T(8,128)(2,1)}, bf16[1,128,2048]{2,1,0:T(8,128)(2,1)}, bf16[1,128,2048]{2,1,0:T(8,128)(2,1)}, bf16[192,1536]{1,0:T(8,128)(2,1)}) custom-call(bf16[1,128,2048]{2,1,0:T(8,128)(2,1)} %get-tuple-element.8.refs_0_, bf16[1,128,2048]{2,1,0:T(8,128)(2,1)} %get-tuple-element.9.refs_1_, ...), custom_call_target="tpu_custom_call" | custom-call | tf_op jit(solution)/shard_map/pallas_call | solution.py:355

commit v4 on v3

--- a/solution.py
+++ b/solution.py
@@ -40,8 +40,8 @@
 def kernel(
     q_ref, k_ref, v_ref, g_ref, drift_ref, idx_ref, crow_ref, crowt_ref, ccol_ref,
     dq_ref, dk_ref, dv_ref, outer_ref,
-    inb, outb, kt_buf, dk_acc, dv_acc, drift_buf, idx_buf, crow, crowt, ccol, kept, picked, place, wide, outer_buf,
-    ss_in, rs_kv, rs_q, rs_g, ss_out, rs_out, ss_kept, rs_kept, lsem,
+    stage, inb, outb, kt_buf, dk_acc, dv_acc, drift_buf, idx_buf, crow, crowt, ccol, kept, picked, place, wide, outer_buf,
+    ss_in, rs_kv, rs_q, ss_out, rs_out, ss_kept, rs_kept, lsem,
 ):
     rep = lax.axis_index("replica")
     seq = lax.axis_index("seq")
@@ -52,7 +52,7 @@
     zlo = (rep // 2) % 4
     core = rep % 2
     m = x * 2 + core
-    ins = (q_ref, k_ref, v_ref, g_ref)
+    ins = (k_ref, v_ref, q_ref, g_ref)
     outs = (dq_ref, dk_ref, dv_ref)
 
     def rep_z(k):
@@ -86,20 +86,28 @@
     for c in locals_:
         c.start()
 
-    def arrival(a):
-        return (rs_q.at[mine], rs_kv.at[0], rs_kv.at[1], rs_g.at[mine])[a]
+    def stage_for(i, carry):
+        for a in range(4):
+            pltpu.make_async_copy(ins[a].at[0, :, cols_of(i)], stage.at[a, i], lsem.at[6]).start()
+        return carry
+
+    lax.fori_loop(0, NWIN, stage_for, 0)
+
+    def arrival(group):
+        return (rs_kv.at[0], rs_q.at[mine])[group]
 
     for a in range(4):
-        pltpu.make_async_copy(ins[a].at[0, :, cols_of(mine)], inb.at[a, rows_of(mine), :], arrival(a)).start()
-
+        pltpu.make_async_copy(ins[a].at[0, :, cols_of(mine)], inb.at[a, rows_of(mine), :], arrival(a // 2)).start()
+
+    pltpu.make_async_copy(stage, stage, lsem.at[6]).wait()
     pl.semaphore_wait(barrier, 7 + 3 + 7)
 
-    def send(a, to):
+    def send(group, to):
         pltpu.make_async_remote_copy(
-            src_ref=ins[a].at[0, :, cols_of(to)],
-            dst_ref=inb.at[a, rows_of(mine), :],
-            send_sem=ss_in.at[a],
-            recv_sem=arrival(a),
+            src_ref=stage.at[2 * group : 2 * group + 2, to],
+            dst_ref=inb.at[2 * group : 2 * group + 2, rows_of(mine), :],
+            send_sem=ss_in.at[group],
+            recv_sem=arrival(group),
             device_id={"seq": base + to},
             device_id_type=MESH,
         ).start()
@@ -107,19 +115,17 @@
     mate = pair * 2 + 1 - mine % 2
 
     def others(group):
-        for a in group:
-            send(a, mate)
+        send(group, mate)
 
         def more(n, carry):
             to = ((pair + 4 - n // 2) % 4) * 2 + n % 2
-            for a in group:
-                send(a, to)
+            send(group, to)
             return carry
 
         lax.fori_loop(2, NWIN, more, 0)
 
-    others((1, 2))
-    others((0, 3))
+    others(0)
+    others(1)
 
     for c in locals_:
         c.wait()
@@ -191,11 +197,10 @@
                 device_id_type=MESH,
             ).start()
 
-    for a in (1, 2):
-        pltpu.make_async_copy(inb.at[a], inb.at[a], rs_kv.at[a - 1]).wait()
+    pltpu.make_async_copy(inb.at[0:2], inb.at[0:2], rs_kv.at[0]).wait()
     for h in range(2):
         of_head = slice(h * HEAD, (h + 1) * HEAD)
-        kt_buf[h] = jnp.transpose(inb[1, :, of_head].astype(F32)).astype(BF16)
+        kt_buf[h] = jnp.transpose(inb[0, :, of_head].astype(F32)).astype(BF16)
     dk_acc[...] = jnp.zeros_like(dk_acc)
     dv_acc[...] = jnp.zeros_like(dv_acc)
 
@@ -214,19 +219,18 @@
         b = (pair + n) % 4
         for u in range(2):
             i = b * 2 + u
-            pltpu.make_async_copy(inb.at[0, rows_of(i)], inb.at[0, rows_of(i)], rs_q.at[i]).wait()
-            pltpu.make_async_copy(inb.at[3, rows_of(i)], inb.at[3, rows_of(i)], rs_g.at[i]).wait()
+            pltpu.make_async_copy(inb.at[2:4, rows_of(i)], inb.at[2:4, rows_of(i)], rs_q.at[i]).wait()
         rows = pl.ds(pl.multiple_of(b * QB, QB), QB)
         for h in range(2):
             of_head = slice(h * HEAD, (h + 1) * HEAD)
-            qb = inb[0, rows, of_head]
+            qb = inb[2, rows, of_head]
             gb = inb[3, rows, of_head]
-            s = lax.dot_general(inb[1, :, of_head], qb, nt, preferred_element_type=F32)
+            s = lax.dot_general(inb[0, :, of_head], qb, nt, preferred_element_type=F32)
             top = jnp.max(s, axis=0, keepdims=True)
             e = jnp.exp((s - top) * scale)
             p = e * (1.0 / jnp.sum(e, axis=0, keepdims=True))
             low = p.astype(BF16)
-            d = lax.dot_general(inb[2, :, of_head], gb, nt, preferred_element_type=F32)
+            d = lax.dot_general(inb[1, :, of_head], gb, nt, preferred_element_type=F32)
             delta = jnp.sum(low.astype(F32) * d, axis=0, keepdims=True)
             sg = (p * (d - delta)).astype(BF16)
             dqt = jnp.dot(kt_buf[h], sg, preferred_element_type=F32) * scale
@@ -288,8 +292,8 @@
     last.start()
 
     part = pl.ds(0, 7 * WIDE)
-    for a in range(4):
-        pltpu.make_async_copy(ins[a].at[0, :, part], ins[a].at[0, :, part], ss_in.at[a]).wait()
+    for group in range(2):
+        pltpu.make_async_copy(stage.at[0:2, 0:7], stage.at[0:2, 0:7], ss_in.at[group]).wait()
     pltpu.make_async_copy(kept.at[0, 0:3], kept.at[0, 0:3], ss_kept.at[0]).wait()
     pltpu.make_async_copy(kept.at[0:7], kept.at[0:7], ss_kept.at[1]).wait()
     for a in range(3):
@@ -323,6 +327,7 @@
         in_specs=[anyspec] * 9,
         out_specs=[anyspec] * 4,
         scratch_shapes=[
+            pltpu.VMEM((4, NWIN, TOK, WIDE), BF16),
             pltpu.VMEM((4, LEN, WIDE), BF16),
             pltpu.VMEM((3, LEN, WIDE), BF16),
             pltpu.VMEM((2, HEAD, LEN), BF16),
@@ -338,15 +343,14 @@
             pltpu.VMEM((32, 24, LANES), F32),
             pltpu.VMEM((32, 24, LANES), F32),
             pltpu.VMEM((ROWS, COLS), BF16),
-            pltpu.SemaphoreType.DMA((4,)),
             pltpu.SemaphoreType.DMA((2,)),
-            pltpu.SemaphoreType.DMA((NWIN,)),
+            pltpu.SemaphoreType.DMA((1,)),
             pltpu.SemaphoreType.DMA((NWIN,)),
             pltpu.SemaphoreType.DMA((3,)),
             pltpu.SemaphoreType.DMA((3,)),
             pltpu.SemaphoreType.DMA((2,)),
             pltpu.SemaphoreType.DMA((2,)),
-            pltpu.SemaphoreType.DMA((6,)),
+            pltpu.SemaphoreType.DMA((7,)),
         ],
         compiler_params=pltpu.CompilerParams(
             collective_id=0, has_side_effects=True, vmem_limit_bytes=63 << 20

time: 182 us -> 182 us (level)
  no operation moved by 1% of the time
where the time goes in v4:
time: 182 us
  Pallas kernels  181 us (99%)
    pallas_call x1, Pallas kernels, on_device(): pl.pallas_call(kernel, out_shape=results, in_specs=[anyspec] * 9, out_spe...  179 us

profile of v4, /device:TPU:1, one launch (start us, length us, event | category | flops | bytes accessed | tf_op | source)
XLA Modules:
  0.0 181.9 jit_solution(17534576233823388699)
XLA Ops:
  0.6 178.8 %shard_map.120 = (bf16[1,128,2048]{2,1,0:T(8,128)(2,1)}, bf16[1,128,2048]{2,1,0:T(8,128)(2,1)}, bf16[1,128,2048]{2,1,0:T(8,128)(2,1)}, bf16[192,1536]{1,0:T(8,128)(2,1)}) custom-call(bf16[1,128,2048]{2,1,0:T(8,128)(2,1)} %q_ref.1, bf16[1,128,2048]{2,1,0:T(8,128)(2,1)} %k_ref.1, bf16[1,128,2048]{2,1,0:T(8,128)(2,1)} %v_ref.1, bf16[1,128,2048]{2,1,0:T(8,128)(2,1)} %g_ref.1, ...), custom_call_target="tpu_custom_call" | custom-call | tf_op jit(solution)/shard_map/pallas_call | solution.py:324
  179.5 2.4 %shard_map.121 = (bf16[1,128,2048]{2,1,0:T(8,128)(2,1)}, bf16[1,128,2048]{2,1,0:T(8,128)(2,1)}, bf16[1,128,2048]{2,1,0:T(8,128)(2,1)}, bf16[192,1536]{1,0:T(8,128)(2,1)}) custom-call(bf16[1,128,2048]{2,1,0:T(8,128)(2,1)} %get-tuple-element.8.refs_0_, bf16[1,128,2048]{2,1,0:T(8,128)(2,1)} %get-tuple-element.9.refs_1_, ...), custom_call_target="tpu_custom_call" | custom-call | tf_op jit(solution)/shard_map/pallas_call | solution.py:359
